TPU v7x, 1024 devices: a whole 4x4x32 slice. The times are simulated.
1024 devices in a mesh: elem: 128 (over y, z), grp: 8 (over x, core).
Axes of the slice: x: 4, y: 4, z: 32, core: 2. Of those that a mesh axis runs over, the one named last changes fastest.
Arguments:
- prognostic: float32 [2, 32768, 16, 128], P(None, ('elem', 'grp')), may hold values from -6 to 6
- wind_field: float32 [2, 32768, 16, 128], P(None, ('elem', 'grp')), may hold values from -6 to 6
- nbr_slot: int32 [32768, 4], P(('elem', 'grp')), may hold values from 0 to 95
- nbr_edge: int32 [32768, 4], P(('elem', 'grp')), may hold values from 0 to 3
- flip_edge: int32 [32768, 4], P(('elem', 'grp')), may hold values from 0 to 1
- span_dest: int32 [524288, 1], P(('elem', 'grp')), may hold values from 0 to 7; in each aligned block of 512 rows (0 to 511, 512 to 1023, ...) at most 128 rows name the same one
- wet_layers_present: int32 [524288], P(('elem', 'grp')), may hold values from 1 to 128
Outputs:
- dynamics_state: float32 [2, 32768, 16, 128], P(None, ('elem', 'grp'))
- tendency: float32 [2, 32768, 16, 128], P(None, ('elem', 'grp'))
- span_rain: float32 [1024], P(('elem', 'grp'))
- cfl_count: float32 [], replicated
Inputs may be any that keep to these rules, and one draw needn't show every extreme that they name: `span_dest`: within the 512 columns of one device at most 128 name the same span, a bound that some block reaches.
All inputs are finite; a program needn't handle non-finite values.
Results may differ from a plain program's by a relative error of at most 0.0003.
Values sent between devices are 32-bit elements; how exact they have to be, the bound alone decides.
A program may use at most 32 MiB of HBM per device.

v0:
```python
import math

import jax
import jax.numpy as jnp
import numpy as np
from jax import lax
from jax.sharding import PartitionSpec as P

STEPS = 2


edge_nodes = np.array([[0, 1, 2, 3], [3, 7, 11, 15], [12, 13, 14, 15], [0, 4, 8, 12]])
time_step = 0.02
viscosity = 0.05
penalty = 4.0
cfl_limit = 2.0
latent = 1.5
evap_rate = 0.02


def padded(cells, sides, width):
    for axis, dim in sides:
        count = lax.axis_size(axis)
        head = lax.slice_in_dim(cells, 0, width, axis=dim)
        tail = lax.slice_in_dim(cells, cells.shape[dim] - width, cells.shape[dim], axis=dim)
        cells = jnp.concatenate(
            [
                lax.ppermute(tail, axis, [(i, (i + 1) % count) for i in range(count)]),
                cells,
                lax.ppermute(head, axis, [((i + 1) % count, i) for i in range(count)]),
            ],
            axis=dim,
        )
    return cells


def nodal_derivative_matrix():
    points = np.array([-1.0, -1.0 / math.sqrt(5.0), 1.0 / math.sqrt(5.0), 1.0])
    off_diag = points[:, None] - points[None, :] + np.eye(4)
    weights = 1.0 / np.prod(off_diag, axis=1)
    derivative = weights[None, :] / weights[:, None] / off_diag
    derivative = derivative * (1.0 - np.eye(4))
    return derivative - np.eye(4) * np.sum(derivative, axis=1)[:, None]


def advance(fields, wind_field, jump_term):
    elements = fields.shape[1]
    layer_total = fields.shape[-1]
    shaped = fields.reshape(2, elements, 4, 4, layer_total)
    derivative = jnp.asarray(nodal_derivative_matrix(), jnp.float32)
    second = jnp.asarray(nodal_derivative_matrix() @ nodal_derivative_matrix(), jnp.float32)
    highest = lax.Precision.HIGHEST
    grad_col = jnp.einsum("ab,zerbl->zeral", derivative, shaped, precision=highest)
    grad_row = jnp.einsum("ab,zebcl->zeacl", derivative, shaped, precision=highest)
    laplace = jnp.einsum("ab,zerbl->zeral", second, shaped, precision=highest)
    laplace = laplace + jnp.einsum("ab,zebcl->zeacl", second, shaped, precision=highest)
    grad_col = grad_col.reshape(fields.shape)
    grad_row = grad_row.reshape(fields.shape)
    laplace = laplace.reshape(fields.shape)
    rate = -(wind_field[0][None] * grad_col + wind_field[1][None] * grad_row) + viscosity * laplace
    for edge_side in range(4):
        rate = rate.at[:, :, edge_nodes[edge_side], :].add(penalty * jump_term[:, :, edge_side])
    return fields + time_step * rate


def vertical_profile_update(thermal_state_kelvin, humidity_mixing_ratio, wet_layers_present):
    layer_total = thermal_state_kelvin.shape[-1]
    heights = jnp.arange(layer_total)
    level_mask = (heights < wet_layers_present[..., None]).astype(jnp.float32)
    condensing_threshold = 0.5 * jnp.exp(0.3 * thermal_state_kelvin)
    condense = (
        0.5 * jax.nn.softplus(2.0 * (humidity_mixing_ratio - condensing_threshold)) * level_mask
    )
    above_mask = (heights[:, None] > heights[None, :]).astype(jnp.float32)
    rain_flux = jnp.matmul(condense, above_mask, precision=lax.Precision.HIGHEST)
    evaporate = evap_rate * rain_flux * level_mask
    warming_source = latent * (condense - evaporate)
    drying = evaporate - condense
    column_rain = jnp.sum(condense - evaporate, axis=-1)
    return (warming_source, drying, column_rain)


def shards(prognostic, wind_field, nbr_slot, nbr_edge, flip_edge, span_dest, wet_layers_present):
    blocks = prognostic.shape[1]
    columns = blocks * 16
    groups = lax.axis_size("grp")
    fields = prognostic
    for dyn_step in range(STEPS):
        traces = fields[:, :, edge_nodes, :]
        halo_pool = padded(traces, (("elem", 1),), blocks)
        across = halo_pool[:, nbr_slot, nbr_edge]
        across = jnp.where(flip_edge[None, :, :, None, None] == 1, across[..., ::-1, :], across)
        fields = advance(fields, wind_field, across - traces)
    lowest_level = jnp.abs(wind_field[0, :, :, 0]) + jnp.abs(wind_field[1, :, :, 0])
    local_count = jnp.sum((lowest_level > cfl_limit).astype(jnp.float32))
    cfl_count = lax.psum(local_count, ("elem", "grp"))
    destination = span_dest[:, 0]
    warming_source, drying, column_rain = vertical_profile_update(
        fields[0], fields[1], wet_layers_present.reshape(blocks, 16)
    )
    tendency = jnp.stack([warming_source, drying])
    one_hot = (destination[:, None] == jnp.arange(groups)[None, :]).astype(jnp.float32)
    partial_rain = jnp.dot(column_rain.reshape(-1), one_hot, precision=lax.Precision.HIGHEST)
    span_rain = lax.psum_scatter(partial_rain, "grp", scatter_dimension=0, tiled=True) / columns
    return (fields, tendency, span_rain, cfl_count)


def solution(mesh):
    in_specs = (
        P(None, ("elem", "grp"), None, None),
        P(None, ("elem", "grp"), None, None),
        P(("elem", "grp"), None),
        P(("elem", "grp"), None),
        P(("elem", "grp"), None),
        P(("elem", "grp"), None),
        P(("elem", "grp")),
    )
    out_specs = (
        P(None, ("elem", "grp"), None, None),
        P(None, ("elem", "grp"), None, None),
        P(("elem", "grp")),
        P(),
    )
    return jax.shard_map(shards, mesh=mesh, in_specs=in_specs, out_specs=out_specs, check_vma=False)
```

profile of v0, /device:TPU:1, one launch (start us, length us, event | category | flops | bytes accessed | tf_op | source)
XLA Modules:
  0.0 252.5 jit_solution(872580059463916646)
XLA Ops:
  1.3 2.0 gather_fusion
  3.4 4.5 %collective-permute-start = (f32[2,32,4,4,128]{4,3,2,1,0:T(4,128)S(1)}, f32[2,32,4,4,128]{4,3,2,1,0:T(4,128)}, u32[]{:S(2)}, u32[]{:S(2)}) collective-permute-start(f32[2,32,4,4,128]{4,3,2,1,0:T(4,128)S(1)} %bitcast.131), channel_id=1, source_target_pairs={{0,8},{8,16},{16,24},{24,32},{32,40},{40,48},{48,56},{56,64},{64,7... | collective-permute-start | bytes 1572872 | tf_op jit(solution)/shard_map/ppermute | solution.py:28
  7.9 19.2 %collective-permute-start.1 = (f32[2,32,4,4,128]{4,3,2,1,0:T(4,128)S(1)}, f32[2,32,4,4,128]{4,3,2,1,0:T(4,128)}, u32[]{:S(2)}, u32[]{:S(2)}) collective-permute-start(f32[2,32,4,4,128]{4,3,2,1,0:T(4,128)S(1)} %bitcast.132), channel_id=1, source_target_pairs={{8,0},{16,8},{24,16},{32,24},{40,32},{48,40},{56,48},{64,56},{72,6... | collective-permute-start | bytes 1572872 | tf_op jit(solution)/shard_map/ppermute | solution.py:30
  29.9 1.1 fusion.3
  32.5 1.1 copy.147
  34.5 1.0 fusion.44
  35.9 1.0 collective-permute-done
  37.7 2.7 %pad_maximum_fusion = f32[2,96,4,4,128]{4,3,2,1,0:T(4,128)} fusion(f32[2,32,4,4,128]{4,3,2,1,0:T(4,128)} %collective-permute-done.1, f32[2,32,4,4,128]{4,3,2,1,0:T(4,128)S(1)} %bitcast.133, f32[2,32,4,4,128]{4,3,2,1,0:T(4,128)} %collective-permute-done), kind=kLoop, calls=%fused_computation.12 | loop fusion | flops 786432 | bytes 3145728 | tf_op jit(solution)/shard_map/concatenate | solution.py:26
  40.4 2.5 gather_fusion.1
  43.0 1.3 rev.6
  44.3 1.4 select_subtract_fusion.1
  50.3 1.9 collective-permute-start.2
  52.2 7.7 %collective-permute-start.3 = (f32[2,32,4,4,128]{4,3,2,1,0:T(4,128)S(1)}, f32[2,32,4,4,128]{4,3,2,1,0:T(4,128)S(1)}, u32[]{:S(2)}, u32[]{:S(2)}) collective-permute-start(f32[2,32,4,4,128]{4,3,2,1,0:T(4,128)S(1)} %bitcast.140), channel_id=1, source_target_pairs={{8,0},{16,8},{24,16},{32,24},{40,32},{48,40},{56,48},{64,56},{72,6... | collective-permute-start | bytes 1572872 | tf_op jit(solution)/shard_map/ppermute | solution.py:30
  60.0 1.0 convolution_bitcast_fusion.1
  61.0 1.0 fusion.11
  62.2 1.1 fusion.1
  63.3 1.0 fusion.45
  64.7 3.8 %collective-permute-done.2 = f32[2,32,4,4,128]{4,3,2,1,0:T(4,128)S(1)} collective-permute-done((f32[2,32,4,4,128]{4,3,2,1,0:T(4,128)S(1)}, f32[2,32,4,4,128]{4,3,2,1,0:T(4,128)S(1)}, u32[]{:S(2)}, u32[]{:S(2)}) %collective-permute-start.2) | collective-permute-done | bytes 524320 | tf_op jit(solution)/shard_map/ppermute | solution.py:28
  69.8 1.8 gather_fusion.3
  71.6 1.1 copy.137
  78.3 1.3 dynamic-slice
  79.6 156.5 %psum.7 = f32[]{:T(128)} all-reduce(f32[]{:T(128)} %convert_reduce_fusion), channel_id=1, replica_groups=mesh['elem'=128,'grp'=8] {'elem','grp'}, use_global_device_ids=true, to_apply=%region_11.12 | all-reduce | flops 1 | bytes 8 | tf_op jit(solution)/shard_map/psum | solution.py:96
  236.1 12.4 %all-reduce = f32[8]{0:T(128)S(1)} all-reduce(f32[8]{0:T(128)S(1)} %convolution_bitcast_fusion.4), channel_id=2, replica_groups=mesh['elem'=128,'grp'=8] {'grp'}, use_global_device_ids=true, to_apply=%region_9.10.clone | all-reduce | flops 8 | bytes 64
  249.4 1.3 dynamic-slice.1
  (81 shorter events, 19.5 us)
Async XLA Ops:
  1.3 25.8 %copy-start.1 = (f32[2,32,16,128]{3,2,1,0:T(8,128)S(1)}, f32[2,32,16,128]{3,2,1,0:T(8,128)}, u32[]{:S(2)}) copy-start(f32[2,32,16,128]{3,2,1,0:T(8,128)} %param.31) | copy-start | bytes 1572868
  3.3 25.3 %copy-start.8 = (s32[32,4]{0,1:T(4,128)S(1)}, s32[32,4]{0,1:T(4,128)}, u32[]{:S(2)}) copy-start(s32[32,4]{0,1:T(4,128)} %param.32) | copy-start | bytes 1540
  3.3 25.3 %copy-start.9 = (s32[32,4]{0,1:T(4,128)S(1)}, s32[32,4]{0,1:T(4,128)}, u32[]{:S(2)}) copy-start(s32[32,4]{0,1:T(4,128)} %param.33) | copy-start | bytes 1540
  3.3 25.5 %copy-start.11 = (s32[32,4]{0,1:T(4,128)S(1)}, s32[32,4]{0,1:T(4,128)}, u32[]{:S(2)}) copy-start(s32[32,4]{0,1:T(4,128)} %param.34) | copy-start | bytes 1540
  3.3 25.6 %copy-start = (f32[2,32,16,128]{3,2,1,0:T(8,128)S(1)}, f32[2,32,16,128]{3,2,1,0:T(8,128)}, u32[]{:S(2)}) copy-start(f32[2,32,16,128]{3,2,1,0:T(8,128)} %param.30) | copy-start | bytes 1572868
  3.3 25.6 %copy-start.5 = (f32[4,4,1,1,1]{1,0,4,3,2:T(4,128)S(1)}, f32[4,4,1,1,1]{1,0,4,3,2:T(4,128)}, u32[]{:S(2)}) copy-start(f32[4,4,1,1,1]{1,0,4,3,2:T(4,128)} %constant.109) | copy-start | bytes 196
  3.4 33.6 %collective-permute-start = (f32[2,32,4,4,128]{4,3,2,1,0:T(4,128)S(1)}, f32[2,32,4,4,128]{4,3,2,1,0:T(4,128)}, u32[]{:S(2)}, u32[]{:S(2)}) collective-permute-start(f32[2,32,4,4,128]{4,3,2,1,0:T(4,128)S(1)} %bitcast.131), channel_id=1, source_target_pairs={{0,8},{8,16},{16,24},{24,32},{32,40},{40,48},{48,56},{56,64},{64,7... | collective-permute-start | bytes 1572872 | tf_op jit(solution)/shard_map/ppermute | solution.py:28
  7.9 29.8 %collective-permute-start.1 = (f32[2,32,4,4,128]{4,3,2,1,0:T(4,128)S(1)}, f32[2,32,4,4,128]{4,3,2,1,0:T(4,128)}, u32[]{:S(2)}, u32[]{:S(2)}) collective-permute-start(f32[2,32,4,4,128]{4,3,2,1,0:T(4,128)S(1)} %bitcast.132), channel_id=1, source_target_pairs={{8,0},{16,8},{24,16},{32,24},{40,32},{48,40},{56,48},{64,56},{72,6... | collective-permute-start | bytes 1572872 | tf_op jit(solution)/shard_map/ppermute | solution.py:30
  28.6 2.5 copy-start.4
  31.1 1.3 copy-start.2
  31.1 1.4 copy-start.10
  45.7 1.0 copy-start.7
  45.7 1.7 copy-start.6
  50.3 18.2 %collective-permute-start.2 = (f32[2,32,4,4,128]{4,3,2,1,0:T(4,128)S(1)}, f32[2,32,4,4,128]{4,3,2,1,0:T(4,128)S(1)}, u32[]{:S(2)}, u32[]{:S(2)}) collective-permute-start(f32[2,32,4,4,128]{4,3,2,1,0:T(4,128)S(1)} %bitcast.139), channel_id=1, source_target_pairs={{0,8},{8,16},{16,24},{24,32},{32,40},{40,48},{48,56},{56,64},{64,7... | collective-permute-start | bytes 1572872 | tf_op jit(solution)/shard_map/ppermute | solution.py:28
  52.2 17.2 %collective-permute-start.3 = (f32[2,32,4,4,128]{4,3,2,1,0:T(4,128)S(1)}, f32[2,32,4,4,128]{4,3,2,1,0:T(4,128)S(1)}, u32[]{:S(2)}, u32[]{:S(2)}) collective-permute-start(f32[2,32,4,4,128]{4,3,2,1,0:T(4,128)S(1)} %bitcast.140), channel_id=1, source_target_pairs={{8,0},{16,8},{24,16},{32,24},{40,32},{48,40},{56,48},{64,56},{72,6... | collective-permute-start | bytes 1572872 | tf_op jit(solution)/shard_map/ppermute | solution.py:30
  77.2 172.2 %copy-start.3 = (f32[2,32,16,128]{3,2,1,0:T(8,128)}, f32[2,32,16,128]{3,2,1,0:T(8,128)S(1)}, u32[]{:S(2)}) copy-start(f32[2,32,16,128]{3,2,1,0:T(8,128)S(1)} %fusion.5) | copy-start | bytes 1572868
  77.2 0.8 copy-start.12
where the time goes:
time: 253 us
  blocking collectives  169 us (67%)
  starting transfers between devices  33.4 us (13%)
  local copies, waits for them, and re-layouts  17 us (7%)
  other arithmetic  14.4 us (6%)
  matrix products  9.25 us (4%)
  waiting for transfers between devices  6.49 us (3%)
  between operations  3.01 us (1%)
    psum x1, blocking collectives, shards(): cfl_count = lax.psum(local_count, ('elem', 'grp'))  157 us
    ppermute x2, starting transfers between devices, padded(): lax.ppermute(head, axis, [((i + 1) % count, i) for i in range(count)])  26.9 us
    unnamed x1, blocking collectives  12.4 us
    ppermute x2, starting transfers between devices, padded(): lax.ppermute(tail, axis, [(i, (i + 1) % count) for i in range(count)])  6.43 us
    scatter-add x8, other arithmetic, advance(): rate.at[:, :, edge_nodes[edge_side], :]  5.89 us
    gather x4, local copies, waits for them, and re-layouts, shards(): across = halo_pool[:, nbr_slot, nbr_edge]  5.5 us
  transfers between devices with their start and end apart: 4, of which 4 were waited for; matrix products, arithmetic and copies ran while one was open for 5% of the time, Pallas kernels for 0%

commit v1 on v0

v1 whole, which is shorter than its diff:
```python
import math

import jax
import jax.numpy as jnp
import numpy as np
from jax import lax
from jax.experimental import pallas as pl
from jax.experimental.pallas import tpu as pltpu
from jax.sharding import PartitionSpec as P

STEPS = 2
ELEMS = 32
ROWS = 512
LEV = 128
EDGE_ROWS = 384

edge_nodes = np.array([[0, 1, 2, 3], [3, 7, 11, 15], [12, 13, 14, 15], [0, 4, 8, 12]])
time_step = 0.02
viscosity = 0.05
penalty = 4.0
cfl_limit = 2.0
latent = 1.5
evap_rate = 0.02

ORDER = [0, 1, 2, 3, 4, 7, 8, 11, 12, 13, 14, 15, 5, 6, 9, 10]
PLACE = {n: p for p, n in enumerate(ORDER)}
EDGE_PLACE = [[PLACE[int(n)] for n in nodes] for nodes in edge_nodes]
SIDES = {n: [(s, i) for s in range(4) for i in range(4) if edge_nodes[s][i] == n] for n in range(16)}

Z_CHIPS = 32
MESH = pl.DeviceIdType.MESH


def nodal_derivative_matrix():
    points = np.array([-1.0, -1.0 / math.sqrt(5.0), 1.0 / math.sqrt(5.0), 1.0])
    off_diag = points[:, None] - points[None, :] + np.eye(4)
    weights = 1.0 / np.prod(off_diag, axis=1)
    derivative = weights[None, :] / weights[:, None] / off_diag
    derivative = derivative * (1.0 - np.eye(4))
    return derivative - np.eye(4) * np.sum(derivative, axis=1)[:, None]


D1 = nodal_derivative_matrix()
D2 = D1 @ D1


def weighted(coefs, values):
    total = None
    for coef, value in zip(coefs, values):
        if abs(coef) < 1e-12:
            continue
        term = value * np.float32(coef)
        total = term if total is None else total + term
    return total


def split_rows(src, dst, rows):
    step = 64

    def body(k, carry):
        at = pl.ds(pl.multiple_of(k * step, step), step)
        x = src[at, :]
        high = x.astype(jnp.bfloat16)
        dst[at, 0:LEV] = high
        dst[at, LEV : 2 * LEV] = (x - high.astype(jnp.float32)).astype(jnp.bfloat16)
        return carry

    lax.fori_loop(0, rows // step, body, 0)


def local_step(src, wind, base, f):
    def body(k, carry):
        at = lambda n: pl.ds(pl.multiple_of(PLACE[n] * ELEMS + k * 8, 8), 8)
        F = [src[f, at(n), :] for n in range(16)]
        for n in range(16):
            r, c = divmod(n, 4)
            row = [F[4 * r + b] for b in range(4)]
            col = [F[4 * b + c] for b in range(4)]
            u = wind[0, pl.ds(k * 128 + n, 8, stride=16), :]
            v = wind[1, pl.ds(k * 128 + n, 8, stride=16), :]
            grad_col = weighted(D1[c] * -time_step, row)
            grad_row = weighted(D1[r] * -time_step, col)
            centre = 1.0 - time_step * penalty * len(SIDES[n])
            centre = centre + time_step * viscosity * (D2[c][c] + D2[r][r])
            others = [b for b in range(4) if b != c]
            others_r = [b for b in range(4) if b != r]
            lap = weighted(
                [centre]
                + [time_step * viscosity * D2[c][b] for b in others]
                + [time_step * viscosity * D2[r][b] for b in others_r],
                [F[n]] + [row[b] for b in others] + [col[b] for b in others_r],
            )
            base[f, at(n), :] = lap + u * grad_col + v * grad_row
        return carry

    lax.fori_loop(0, ELEMS // 8, body, 0)


def sum_rows(x):
    return jnp.sum(x, axis=0, keepdims=True)


def kernel(
    prog, wind, slot, edge, flip, dest, wet,
    dyn, tend, rain, cfl,
    praw, wraw, islot, iedge, iflip, idest, iwet,
    p0, p1, base, recv, jm, rhs, rhs_own, tq, bt, cols, cond, condf, obuf, tbuf,
    cval, crecv, part, precv,
    in_sem, hs_sem, hr_sem, cs_sem, cr_sem, rs_sem, rr_sem, out_sem,
):
    f32, bf16 = jnp.float32, jnp.bfloat16
    me = lax.axis_index("elem")
    grp = lax.axis_index("grp")
    n_elem = lax.axis_size("elem")
    nxt, prv = lax.rem(me + 1, n_elem), lax.rem(me + n_elem - 1, n_elem)
    y, z = me // Z_CHIPS, lax.rem(me, Z_CHIPS)
    zh, zl = z // 4, lax.rem(z, 4)
    grp_peers = [(me, lax.rem(grp + k, 8)) for k in range(1, 8)]
    y_peers = [(lax.rem(y + k, 4) * Z_CHIPS + z, grp) for k in range(1, 4)]
    zl_peers = [(y * Z_CHIPS + zh * 4 + lax.rem(zl + k, 4), grp) for k in range(1, 4)]
    zh_peers = [(y * Z_CHIPS + lax.rem(zh + k, 8) * 4 + zl, grp) for k in range(1, 8)]

    loads = [
        pltpu.make_async_copy(src, dst, in_sem.at[i])
        for i, (src, dst) in enumerate(
            [
                (prog.at[0], praw.at[0]),
                (prog.at[1], praw.at[1]),
                (wind, wraw),
                (slot, islot),
                (edge, iedge),
                (flip, iflip),
                (dest, idest),
                (wet, iwet),
            ]
        )
    ]
    for copy in loads:
        copy.start()

    barrier = pltpu.get_barrier_semaphore()
    peers = [(nxt, grp), (prv, grp)] + grp_peers + y_peers + zl_peers + zh_peers
    for peer in peers:
        pl.semaphore_signal(barrier, inc=1, device_id=peer, device_id_type=MESH)

    def pack(f):
        def body(k, carry):
            for n in range(16):
                at = pl.ds(pl.multiple_of(PLACE[n] * ELEMS + k * 8, 8), 8)
                p0[f, at, :] = praw[f, pl.ds(k * 128 + n, 8, stride=16), :]
            return carry

        lax.fori_loop(0, ELEMS // 8, body, 0)

    def halo(step, src, f):
        copies = []
        for way, target in enumerate((nxt, prv)):
            copies.append(
                pltpu.make_async_remote_copy(
                    src_ref=src.at[f, pl.ds(0, EDGE_ROWS)],
                    dst_ref=recv.at[step, f, pl.ds(way * EDGE_ROWS, EDGE_ROWS)],
                    send_sem=hs_sem.at[step, f, way],
                    recv_sem=hr_sem.at[step, f, way],
                    device_id=(target, grp),
                    device_id_type=MESH,
                )
            )
        return copies

    started = []
    halos = [[halo(s, src, f) for f in range(2)] for s, src in enumerate((p0, p1))]

    def send_halo(step, f):
        for copy in halos[step][f]:
            copy.start()
            started.append(copy)

    loads[0].wait()
    pack(0)
    pl.semaphore_wait(barrier, len(peers))
    send_halo(0, 0)
    loads[1].wait()
    pack(1)
    send_halo(0, 1)

    lane = lax.broadcasted_iota(jnp.int32, (8, LEV), 1)

    loads[2].wait()

    def count_body(k, total):
        at = pl.ds(pl.multiple_of(k * 32, 32), 32)
        speed = jnp.abs(wraw[0, at, :]) + jnp.abs(wraw[1, at, :])
        flag = jnp.where(speed > cfl_limit, 1.0, 0.0).astype(f32)
        return total + (flag[0:8] + flag[8:16] + flag[16:24] + flag[24:32])

    count = lax.fori_loop(0, ROWS // 32, count_body, jnp.zeros((8, LEV), f32))
    cval[0] = sum_rows(jnp.where(lane == 0, count, 0.0))

    stages = [(grp_peers, 0), (y_peers, 7), (zl_peers, 10), (zh_peers, 13)]

    def count_send(stage):
        targets, first = stages[stage]
        copies = []
        for k, peer in enumerate(targets):
            copy = pltpu.make_async_remote_copy(
                src_ref=cval.at[stage],
                dst_ref=crecv.at[first + k],
                send_sem=cs_sem.at[first + k],
                recv_sem=cr_sem.at[first + k],
                device_id=peer,
                device_id_type=MESH,
            )
            copy.start()
            copies.append(copy)
            started.append(copy)
        return copies

    def count_sum(stage, copies):
        for copy in copies:
            copy.wait_recv()
        targets, first = stages[stage]
        total = cval[stage]
        for k in range(len(targets)):
            total = total + crecv[first + k]
        return total

    flying = count_send(0)

    local_step(p0, wraw, base, 0)

    for copy in loads[3:]:
        copy.wait()
    s_, e_, f_ = islot[...], iedge[...], iflip[...]
    origin = jnp.where(s_ < ELEMS, 0, jnp.where(s_ < 2 * ELEMS, 2 * EDGE_ROWS, EDGE_ROWS))
    origin = origin + (s_ & (ELEMS - 1))
    facing = []
    for i in range(4):
        place = jnp.full(e_.shape, EDGE_PLACE[0][i], jnp.int32)
        for s in range(1, 4):
            place = jnp.where(e_ == s, EDGE_PLACE[s][i], place)
        facing.append(place)
    tq[...] = jnp.zeros_like(tq)
    for i in range(4):
        target = origin + ELEMS * jnp.where(f_ == 1, facing[3 - i], facing[i])
        low = target & (LEV - 1)
        tq[4 * i : 4 * i + 4, 0:ELEMS] = (target - low).astype(f32)
        tq[16 + 4 * i : 20 + 4 * i, 0:ELEMS] = low.astype(f32)
    wide = (32, 16 * LEV)
    pick = (lax.broadcasted_iota(jnp.int32, wide, 0) & 15) == (lax.broadcasted_iota(jnp.int32, wide, 1) >> 7)
    pick = jnp.where(pick, 1.0, 0.0).astype(bf16)
    bt[...] = lax.dot_general(
        tq[...].astype(bf16), pick, (((0,), (0,)), ((), ())), preferred_element_type=f32
    )[0:ELEMS]

    lanes32 = lax.broadcasted_iota(jnp.int32, (ELEMS, LEV), 1).astype(f32)

    def jm_body(k, carry):
        cell = lanes32 + (k * LEV).astype(f32)
        at = pl.ds(pl.multiple_of(k * LEV, LEV), LEV)
        for place in range(12):
            hit = None
            for s, i in SIDES[ORDER[place]]:
                col = (4 * i + s) * LEV
                one = jnp.where(bt[:, col : col + LEV] == cell, 1.0, 0.0)
                hit = one if hit is None else hit + one
            jm[place * ELEMS : (place + 1) * ELEMS, at] = hit.astype(bf16)
        return carry

    lax.fori_loop(0, 9, jm_body, 0)

    edge_scale = np.float32(time_step * penalty)

    def add_own(src, f):
        split_rows(src.at[f], rhs_own, EDGE_ROWS)
        got = jnp.dot(jm[:, 2 * EDGE_ROWS :], rhs_own[...], preferred_element_type=f32)
        base[f, 0:EDGE_ROWS, :] = base[f, 0:EDGE_ROWS, :] + edge_scale * (got[:, :LEV] + got[:, LEV:])

    def from_halo(step, f):
        for copy in halos[step][f]:
            copy.wait_recv()
        split_rows(recv.at[step, f], rhs, 2 * EDGE_ROWS)
        got = jnp.dot(jm[:, : 2 * EDGE_ROWS], rhs[...], preferred_element_type=f32)
        return edge_scale * (got[:, :LEV] + got[:, LEV:])

    add_own(p0, 0)
    total = count_sum(0, flying)
    cval[1] = total
    flying = count_send(1)
    local_step(p0, wraw, base, 1)
    add_own(p0, 1)

    row32 = lax.broadcasted_iota(jnp.int32, (8, LEV), 0)
    mine = (lane >> 4) == row32
    for j, ref in enumerate((iwet, idest)):
        for q in range(4):
            line = jnp.broadcast_to(ref[q : q + 1, :].astype(f32), (8, LEV))
            tq[8 * q : 8 * q + 8, :] = jnp.where(mine, line, 0.0)
        tall = (LEV, 16 * LEV)
        spread = (lax.broadcasted_iota(jnp.int32, tall, 0) & 15) == (lax.broadcasted_iota(jnp.int32, tall, 1) >> 7)
        spread = jnp.where(spread, 1.0, 0.0).astype(bf16)
        cols[j] = jnp.dot(tq[...].astype(bf16), spread, preferred_element_type=f32)

    for f in range(2):
        p1[f, 0:EDGE_ROWS, :] = base[f, 0:EDGE_ROWS, :] + from_halo(0, f)
        send_halo(1, f)
        p1[f, EDGE_ROWS:, :] = base[f, EDGE_ROWS:, :]
        if f == 0:
            total = count_sum(1, flying)
            cval[2] = total
            flying = count_send(2)
            local_step(p1, wraw, base, 0)
            add_own(p1, 0)
    local_step(p1, wraw, base, 1)
    add_own(p1, 1)
    total = count_sum(2, flying)
    cval[3] = total
    flying = count_send(3)

    stores = []

    def store(src, dst):
        copy = pltpu.make_async_copy(src, dst, out_sem.at[len(stores)])
        copy.start()
        stores.append(copy)

    def to_elements(src, dst, f, k):
        for n in range(16):
            at = pl.ds(pl.multiple_of(PLACE[n] * ELEMS + k * 8, 8), 8)
            dst[f, pl.ds(k * 128 + n, 8, stride=16), :] = src[f, at, :]

    for f in range(2):
        base[f, 0:EDGE_ROWS, :] = base[f, 0:EDGE_ROWS, :] + from_halo(1, f)

        def out_body(k, carry):
            to_elements(base, obuf, f, k)
            return carry

        lax.fori_loop(0, ELEMS // 8, out_body, 0)
        store(obuf.at[f], dyn.at[f])

    for place in range(16):
        at = slice(place * ELEMS, (place + 1) * ELEMS)
        warm, moist = base[0, at, :], base[1, at, :]
        active = cols[0, :, place_lanes(place)]
        x = 2.0 * (moist - 0.5 * jnp.exp(0.3 * warm))
        soft = jnp.maximum(x, 0.0) + jnp.log1p(jnp.exp(-jnp.abs(x)))
        condense = jnp.where(lanes32 < active, 0.5 * soft, 0.0)
        high = condense.astype(bf16)
        condf[at, :] = condense
        cond[at, 0:LEV] = high
        cond[at, LEV:] = (condense - high.astype(f32)).astype(bf16)
    deep = (2 * LEV, LEV)
    above = (lax.broadcasted_iota(jnp.int32, deep, 0) & (LEV - 1)) > lax.broadcasted_iota(jnp.int32, deep, 1)
    above = jnp.where(above, 1.0, 0.0).astype(bf16)
    flux = jnp.dot(cond[...], above, preferred_element_type=f32)
    sums = [jnp.zeros((8, LEV), f32) for _ in range(8)]
    for place in range(16):
        at = slice(place * ELEMS, (place + 1) * ELEMS)
        n = ORDER[place]
        active = cols[0, :, place_lanes(place)]
        owner = cols[1, :, place_lanes(place)]
        condense = condf[at, :]
        net = condense - jnp.where(lanes32 < active, evap_rate * flux[at, :], 0.0)
        warming, drying = latent * net, -net
        for k in range(4):
            spot = pl.ds(k * 128 + n, 8, stride=16)
            tbuf[0, spot, :] = warming[8 * k : 8 * k + 8]
            tbuf[1, spot, :] = drying[8 * k : 8 * k + 8]
        for g in range(8):
            share = jnp.where(owner == float(g), net, 0.0)
            sums[g] = sums[g] + (share[0:8] + share[8:16] + share[16:24] + share[24:32])
    for g in range(8):
        part[g] = sum_rows(sums[g])
    rain_copies = []
    for k, (_, peer) in enumerate(grp_peers):
        copy = pltpu.make_async_remote_copy(
            src_ref=part.at[peer],
            dst_ref=precv.at[k],
            send_sem=rs_sem.at[k],
            recv_sem=rr_sem.at[k],
            device_id=(me, peer),
            device_id_type=MESH,
        )
        copy.start()
        rain_copies.append(copy)
        started.append(copy)
    store(tbuf, tend)

    cfl[0] = jnp.sum(count_sum(3, flying))
    for copy in rain_copies:
        copy.wait_recv()
    collected = part[grp]
    for k in range(7):
        collected = collected + precv[k]
    rain[0] = jnp.sum(collected) * np.float32(1.0 / ROWS)
    for copy in started:
        copy.wait_send()
    for copy in stores:
        copy.wait()


def place_lanes(place):
    n = ORDER[place]
    return slice(n * LEV, (n + 1) * LEV)


def shards(prognostic, wind_field, nbr_slot, nbr_edge, flip_edge, span_dest, wet_layers_present):
    f32 = jnp.float32
    anywhere = pl.BlockSpec(memory_space=pl.ANY)
    scalar = pl.BlockSpec(memory_space=pltpu.SMEM)
    vmem = pltpu.VMEM
    dma = pltpu.SemaphoreType.DMA
    whole = (2, ROWS, LEV)
    fields, tendency, rain, cfl = pl.pallas_call(
        kernel,
        out_shape=(
            jax.ShapeDtypeStruct(whole, f32),
            jax.ShapeDtypeStruct(whole, f32),
            jax.ShapeDtypeStruct((1,), f32),
            jax.ShapeDtypeStruct((1,), f32),
        ),
        in_specs=[anywhere] * 7,
        out_specs=(anywhere, anywhere, scalar, scalar),
        scratch_shapes=[
            vmem(whole, f32),
            vmem(whole, f32),
            vmem((4, ELEMS), jnp.int32),
            vmem((4, ELEMS), jnp.int32),
            vmem((4, ELEMS), jnp.int32),
            vmem((4, LEV), jnp.int32),
            vmem((4, LEV), jnp.int32),
            vmem(whole, f32),
            vmem(whole, f32),
            vmem(whole, f32),
            vmem((2, 2, 2 * EDGE_ROWS, LEV), f32),
            vmem((EDGE_ROWS, 3 * EDGE_ROWS), jnp.bfloat16),
            vmem((2 * EDGE_ROWS, 2 * LEV), jnp.bfloat16),
            vmem((EDGE_ROWS, 2 * LEV), jnp.bfloat16),
            vmem((ELEMS, LEV), f32),
            vmem((ELEMS, 16 * LEV), f32),
            vmem((2, ELEMS, 16 * LEV), f32),
            vmem((ROWS, 2 * LEV), jnp.bfloat16),
            vmem((ROWS, LEV), f32),
            vmem(whole, f32),
            vmem(whole, f32),
            vmem((4, 1, LEV), f32),
            vmem((20, 1, LEV), f32),
            vmem((8, 1, LEV), f32),
            vmem((7, 1, LEV), f32),
            dma((8,)),
            dma((2, 2, 2)),
            dma((2, 2, 2)),
            dma((20,)),
            dma((20,)),
            dma((7,)),
            dma((7,)),
            dma((3,)),
        ],
        compiler_params=pltpu.CompilerParams(
            collective_id=0, has_side_effects=True, vmem_limit_bytes=48 * 1024 * 1024
        ),
        cost_estimate=pl.CostEstimate(flops=2_000_000_000, bytes_accessed=2_200_000, transcendentals=200_000),
        name="steps_and_columns",
    )(
        prognostic.reshape(whole),
        wind_field.reshape(whole),
        nbr_slot.T,
        nbr_edge.T,
        flip_edge.T,
        span_dest.reshape(4, LEV),
        wet_layers_present.reshape(4, LEV),
    )
    shape = prognostic.shape
    return fields.reshape(shape), tendency.reshape(shape), rain, cfl.reshape(())


def solution(mesh):
    in_specs = (
        P(None, ("elem", "grp"), None, None),
        P(None, ("elem", "grp"), None, None),
        P(("elem", "grp"), None),
        P(("elem", "grp"), None),
        P(("elem", "grp"), None),
        P(("elem", "grp"), None),
        P(("elem", "grp")),
    )
    out_specs = (
        P(None, ("elem", "grp"), None, None),
        P(None, ("elem", "grp"), None, None),
        P(("elem", "grp")),
        P(),
    )
    return jax.shard_map(shards, mesh=mesh, in_specs=in_specs, out_specs=out_specs, check_vma=False)
```

time: 253 us -> 65.2 us (0.26)
  blocking collectives: 169 us -> 0 us
  Pallas kernels: 0 us -> 56.4 us
  starting transfers between devices: 33.4 us -> 0 us
  other arithmetic: 14.4 us -> 0 us
  local copies, waits for them, and re-layouts: 17 us -> 4.38 us
  matrix products: 9.25 us -> 0 us
  waiting for transfers between devices: 6.49 us -> 0 us
    psum x1 -> x0, blocking collectives: 157 us -> none  [shards(): cfl_count = lax.psum(local_count, ('elem', 'grp'))]
    pallas_call x0 -> x1, Pallas kernels: none -> 56.4 us  [shards(): pl.pallas_call(kernel, out_shape=(jax.ShapeDtypeStruct(whole, f32), jax.S...]
    ppermute x4 -> x0, starting transfers between devices: 33.4 us -> none  [the longest x2 26.9 us: padded(): lax.ppermute(head, axis, [((i + 1) % count, i) for i in range(count)])]
    unnamed x1 -> x0, blocking collectives: 12.4 us -> none
    dot_general x10 -> x0, matrix products: 9.25 us -> none  [the longest x2 2.22 us: advance(): laplace = jnp.einsum('ab,zerbl->zeral', second, shaped, precision=highest)]
    gather x7 -> x0, local copies, waits for them, and re-layouts: 8.38 us -> none  [the longest x4 5.5 us: shards(): across = halo_pool[:, nbr_slot, nbr_edge]]
    ppermute x4 -> x0, waiting for transfers between devices: 6.49 us -> none  [the longest x2 4.84 us: padded(): lax.ppermute(tail, axis, [(i, (i + 1) % count) for i in range(count)])]
    scatter-add x8 -> x0, other arithmetic: 5.89 us -> none  [advance(): rate.at[:, :, edge_nodes[edge_side], :]]
  transfers between devices with their start and end apart: 4 -> 0, of which waited for: 4 -> 0; matrix products, arithmetic and copies ran while one was open for 5% -> 0% of each run, Pallas kernels for 0% -> 0%
where the time goes in v1:
time: 65.2 us; the launch traced here: 64.9 us
  Pallas kernels  56.4 us (87%)
  local copies, waits for them, and re-layouts  4.38 us (7%)
  between operations  4.18 us (6%)
    pallas_call x1, Pallas kernels, shards(): pl.pallas_call(kernel, out_shape=(jax.ShapeDtypeStruct(whole, f32), jax.S...  56.4 us
    unnamed x16, local copies, waits for them, and re-layouts  4.38 us

profile of v1, /device:TPU:1, one launch (start us, length us, event | category | flops | bytes accessed | tf_op | source)
XLA Modules:
  0.0 64.9 jit_solution(13501117639463406439)
XLA Ops:
  0.6 0.0 copy-start.6
  0.6 0.0 copy-start.5
  0.7 0.0 copy-start.4
  0.7 0.0 copy-start.3
  0.7 0.0 copy-start.2
  0.7 0.6 copy-done.6
  1.3 0.0 copy-done.5
  1.3 0.0 copy-done.4
  1.3 0.0 copy-done.3
  1.4 0.0 copy-done.2
  1.4 0.0 copy-start
  1.4 1.0 %copy-done = f32[2,32,16,128]{3,2,1,0:T(8,128)S(1)} copy-done((f32[2,32,16,128]{3,2,1,0:T(8,128)S(1)}, f32[2,32,16,128]{3,2,1,0:T(8,128)}, u32[]{:S(2)}) %copy-start) | copy-done | bytes 524312
  2.4 0.0 copy-start.1
  2.4 1.0 %copy-done.1 = f32[2,32,16,128]{3,2,1,0:T(8,128)S(1)} copy-done((f32[2,32,16,128]{3,2,1,0:T(8,128)S(1)}, f32[2,32,16,128]{3,2,1,0:T(8,128)}, u32[]{:S(2)}) %copy-start.1) | copy-done | bytes 524312
  3.5 56.4 %steps_and_columns.1 = (f32[2,512,128]{2,1,0:T(8,128)S(1)}, f32[2,512,128]{2,1,0:T(8,128)S(1)}, f32[1]{0:T(128)}, f32[1]{0:T(128)}) custom-call(f32[2,512,128]{2,1,0:T(8,128)S(1)} %bitcast.12, f32[2,512,128]{2,1,0:T(8,128)S(1)} %bitcast.13, s32[4,32]{1,0:T(4,128)S(1)} %bitcast.14, s32[4,32]{1,0:T(4,128)S(1)} %bitcast.15, s32[4,32]{1,0:T(4,128)S(1)} %bitcast.16, ...), custom_call_target="tpu_custom_call" | custom-call | flops 2000000000 | bytes 2200000 | tf_op jit(solution)/shard_map/steps_and_columns/pallas_call | solution.py:414
  59.8 0.8 %copy.15 = f32[2,32,16,128]{3,2,1,0:T(8,128)} copy(f32[2,32,16,128]{3,2,1,0:T(8,128)S(1)} %bitcast.11) | data formatting | bytes 1048576
  60.6 0.8 %copy.16 = f32[2,32,16,128]{3,2,1,0:T(8,128)} copy(f32[2,32,16,128]{3,2,1,0:T(8,128)S(1)} %bitcast.10) | data formatting | bytes 1048576
Async XLA Ops:
  0.6 0.7 %copy-start.6 = (s32[512]{0:T(512)S(1)}, s32[512]{0:T(512)}, u32[]{:S(2)}) copy-start(s32[512]{0:T(512)} %param.13) | copy-start | bytes 6148
  0.6 0.7 %copy-start.5 = (s32[512,1]{0,1:T(1,128)S(1)}, s32[512,1]{0,1:T(1,128)}, u32[]{:S(2)}) copy-start(s32[512,1]{0,1:T(1,128)} %param.12) | copy-start | bytes 6148
  0.7 0.7 %copy-start.4 = (s32[32,4]{0,1:T(4,128)S(1)}, s32[32,4]{0,1:T(4,128)}, u32[]{:S(2)}) copy-start(s32[32,4]{0,1:T(4,128)} %param.11) | copy-start | bytes 1540
  0.7 0.7 %copy-start.3 = (s32[32,4]{0,1:T(4,128)S(1)}, s32[32,4]{0,1:T(4,128)}, u32[]{:S(2)}) copy-start(s32[32,4]{0,1:T(4,128)} %param.10) | copy-start | bytes 1540
  0.7 0.7 %copy-start.2 = (s32[32,4]{0,1:T(4,128)S(1)}, s32[32,4]{0,1:T(4,128)}, u32[]{:S(2)}) copy-start(s32[32,4]{0,1:T(4,128)} %param.9) | copy-start | bytes 1540
  1.4 1.0 %copy-start = (f32[2,32,16,128]{3,2,1,0:T(8,128)S(1)}, f32[2,32,16,128]{3,2,1,0:T(8,128)}, u32[]{:S(2)}) copy-start(f32[2,32,16,128]{3,2,1,0:T(8,128)} %param.7) | copy-start | bytes 1572868
  2.4 1.0 %copy-start.1 = (f32[2,32,16,128]{3,2,1,0:T(8,128)S(1)}, f32[2,32,16,128]{3,2,1,0:T(8,128)}, u32[]{:S(2)}) copy-start(f32[2,32,16,128]{3,2,1,0:T(8,128)} %param.8) | copy-start | bytes 1572868

commit v2 on v1

--- a/solution.py
+++ b/solution.py
@@ -28,6 +28,7 @@
 SIDES = {n: [(s, i) for s in range(4) for i in range(4) if edge_nodes[s][i] == n] for n in range(16)}
 
 Z_CHIPS = 32
+ROOT = 4
 MESH = pl.DeviceIdType.MESH
 
 
@@ -102,11 +103,11 @@
 
 def kernel(
     prog, wind, slot, edge, flip, dest, wet,
-    dyn, tend, rain, cfl,
+    dyn, tend, sums_out,
     praw, wraw, islot, iedge, iflip, idest, iwet,
     p0, p1, base, recv, jm, rhs, rhs_own, tq, bt, cols, cond, condf, obuf, tbuf,
-    cval, crecv, part, precv,
-    in_sem, hs_sem, hr_sem, cs_sem, cr_sem, rs_sem, rr_sem, out_sem,
+    cval, crecv, gsum, ctot, part, precv, lines,
+    in_sem, hs_sem, hr_sem, cs_sem, cr_sem, gs_sem, gr_sem, rs_sem, rr_sem, out_sem,
 ):
     f32, bf16 = jnp.float32, jnp.bfloat16
     me = lax.axis_index("elem")
@@ -114,34 +115,35 @@
     n_elem = lax.axis_size("elem")
     nxt, prv = lax.rem(me + 1, n_elem), lax.rem(me + n_elem - 1, n_elem)
     y, z = me // Z_CHIPS, lax.rem(me, Z_CHIPS)
-    zh, zl = z // 4, lax.rem(z, 4)
     grp_peers = [(me, lax.rem(grp + k, 8)) for k in range(1, 8)]
-    y_peers = [(lax.rem(y + k, 4) * Z_CHIPS + z, grp) for k in range(1, 4)]
-    zl_peers = [(y * Z_CHIPS + zh * 4 + lax.rem(zl + k, 4), grp) for k in range(1, 4)]
-    zh_peers = [(y * Z_CHIPS + lax.rem(zh + k, 8) * 4 + zl, grp) for k in range(1, 8)]
-
-    loads = [
-        pltpu.make_async_copy(src, dst, in_sem.at[i])
-        for i, (src, dst) in enumerate(
-            [
-                (prog.at[0], praw.at[0]),
-                (prog.at[1], praw.at[1]),
-                (wind, wraw),
-                (slot, islot),
-                (edge, iedge),
-                (flip, iflip),
-                (dest, idest),
-                (wet, iwet),
-            ]
-        )
-    ]
+    z_line = [(y * Z_CHIPS + lax.rem(ROOT + k, Z_CHIPS), grp) for k in range(1, Z_CHIPS)]
+    away = lax.rem(z + Z_CHIPS - ROOT, Z_CHIPS)
+    is_root = z == ROOT
+
+    halves = lambda src, dst: [(src.at[pl.ds(k, 256)], dst.at[pl.ds(k, 256)]) for k in (0, 256)]
+    pieces = halves(prog.at[0], praw.at[0])
+    pieces += halves(wind.at[0], wraw.at[0]) + halves(wind.at[1], wraw.at[1])
+    pieces += halves(prog.at[1], praw.at[1])
+    pieces += [(slot, islot), (edge, iedge), (flip, iflip), (dest, idest), (wet, iwet)]
+    loads = [pltpu.make_async_copy(src, dst, in_sem.at[i]) for i, (src, dst) in enumerate(pieces)]
     for copy in loads:
         copy.start()
 
     barrier = pltpu.get_barrier_semaphore()
-    peers = [(nxt, grp), (prv, grp)] + grp_peers + y_peers + zl_peers + zh_peers
-    for peer in peers:
+
+    def greet(peer):
         pl.semaphore_signal(barrier, inc=1, device_id=peer, device_id_type=MESH)
+
+    for peer in [(nxt, grp), (prv, grp)] + grp_peers:
+        greet(peer)
+
+    @pl.when(is_root)
+    def _():
+        def greet_body(k, carry):
+            greet((lax.rem(y + k // Z_CHIPS, 4) * Z_CHIPS + lax.rem(ROOT + lax.rem(k, Z_CHIPS), Z_CHIPS), grp))
+            return carry
+
+        lax.fori_loop(1, 4 * Z_CHIPS, greet_body, 0)
 
     def pack(f):
         def body(k, carry):
@@ -175,17 +177,12 @@
             copy.start()
             started.append(copy)
 
-    loads[0].wait()
-    pack(0)
-    pl.semaphore_wait(barrier, len(peers))
-    send_halo(0, 0)
-    loads[1].wait()
-    pack(1)
-    send_halo(0, 1)
-
+    def arrived(first, last):
+        for copy in loads[first:last]:
+            copy.wait()
+
+    arrived(2, 6)
     lane = lax.broadcasted_iota(jnp.int32, (8, LEV), 1)
-
-    loads[2].wait()
 
     def count_body(k, total):
         at = pl.ds(pl.multiple_of(k * 32, 32), 32)
@@ -195,41 +192,43 @@
 
     count = lax.fori_loop(0, ROWS // 32, count_body, jnp.zeros((8, LEV), f32))
     cval[0] = sum_rows(jnp.where(lane == 0, count, 0.0))
-
-    stages = [(grp_peers, 0), (y_peers, 7), (zl_peers, 10), (zh_peers, 13)]
-
-    def count_send(stage):
-        targets, first = stages[stage]
-        copies = []
-        for k, peer in enumerate(targets):
-            copy = pltpu.make_async_remote_copy(
-                src_ref=cval.at[stage],
-                dst_ref=crecv.at[first + k],
-                send_sem=cs_sem.at[first + k],
-                recv_sem=cr_sem.at[first + k],
-                device_id=peer,
-                device_id_type=MESH,
-            )
-            copy.start()
-            copies.append(copy)
-            started.append(copy)
-        return copies
-
-    def count_sum(stage, copies):
-        for copy in copies:
-            copy.wait_recv()
-        targets, first = stages[stage]
-        total = cval[stage]
-        for k in range(len(targets)):
-            total = total + crecv[first + k]
-        return total
-
-    flying = count_send(0)
+    crecv[0] = cval[0]
+
+    def remote(src, dst, send_sem, recv_sem, peer):
+        return pltpu.make_async_remote_copy(
+            src_ref=src, dst_ref=dst, send_sem=send_sem, recv_sem=recv_sem, device_id=peer, device_id_type=MESH
+        )
+
+    to_root = [
+        remote(
+            cval.at[0],
+            crecv.at[(4 - j) % 4 * Z_CHIPS + away],
+            cs_sem.at[j],
+            cr_sem.at[0],
+            (lax.rem(y + j, 4) * Z_CHIPS + ROOT, grp),
+        )
+        for j in range(4)
+    ]
+
+    arrived(0, 2)
+    pack(0)
+    pl.semaphore_wait(barrier, jnp.where(is_root, 12, 13))
+
+    @pl.when(z != ROOT)
+    def _():
+        to_root[0].start()
+
+    for copy in to_root[1:]:
+        copy.start()
+    started.extend(to_root[1:])
+    send_halo(0, 0)
+    arrived(6, 8)
+    pack(1)
+    send_halo(0, 1)
 
     local_step(p0, wraw, base, 0)
 
-    for copy in loads[3:]:
-        copy.wait()
+    arrived(8, 13)
     s_, e_, f_ = islot[...], iedge[...], iflip[...]
     origin = jnp.where(s_ < ELEMS, 0, jnp.where(s_ < 2 * ELEMS, 2 * EDGE_ROWS, EDGE_ROWS))
     origin = origin + (s_ & (ELEMS - 1))
@@ -283,9 +282,6 @@
         return edge_scale * (got[:, :LEV] + got[:, LEV:])
 
     add_own(p0, 0)
-    total = count_sum(0, flying)
-    cval[1] = total
-    flying = count_send(1)
     local_step(p0, wraw, base, 1)
     add_own(p0, 1)
 
@@ -305,16 +301,10 @@
         send_halo(1, f)
         p1[f, EDGE_ROWS:, :] = base[f, EDGE_ROWS:, :]
         if f == 0:
-            total = count_sum(1, flying)
-            cval[2] = total
-            flying = count_send(2)
             local_step(p1, wraw, base, 0)
             add_own(p1, 0)
     local_step(p1, wraw, base, 1)
     add_own(p1, 1)
-    total = count_sum(2, flying)
-    cval[3] = total
-    flying = count_send(3)
 
     stores = []
 
@@ -328,21 +318,29 @@
             at = pl.ds(pl.multiple_of(PLACE[n] * ELEMS + k * 8, 8), 8)
             dst[f, pl.ds(k * 128 + n, 8, stride=16), :] = src[f, at, :]
 
-    for f in range(2):
-        base[f, 0:EDGE_ROWS, :] = base[f, 0:EDGE_ROWS, :] + from_halo(1, f)
-
-        def out_body(k, carry):
+    def out_field(f):
+        def body(k, carry):
             to_elements(base, obuf, f, k)
             return carry
 
-        lax.fori_loop(0, ELEMS // 8, out_body, 0)
+        lax.fori_loop(0, ELEMS // 8, body, 0)
         store(obuf.at[f], dyn.at[f])
+
+    base[0, 0:EDGE_ROWS, :] = base[0, 0:EDGE_ROWS, :] + from_halo(1, 0)
+    out_field(0)
+
+    def threshold(k, carry):
+        at = pl.ds(pl.multiple_of(k * 32, 32), 32)
+        condf[at, :] = jnp.exp(0.3 * base[0, at, :])
+        return carry
+
+    lax.fori_loop(0, ROWS // 32, threshold, 0)
+    base[1, 0:EDGE_ROWS, :] = base[1, 0:EDGE_ROWS, :] + from_halo(1, 1)
 
     for place in range(16):
         at = slice(place * ELEMS, (place + 1) * ELEMS)
-        warm, moist = base[0, at, :], base[1, at, :]
         active = cols[0, :, place_lanes(place)]
-        x = 2.0 * (moist - 0.5 * jnp.exp(0.3 * warm))
+        x = 2.0 * base[1, at, :] - condf[at, :]
         soft = jnp.maximum(x, 0.0) + jnp.log1p(jnp.exp(-jnp.abs(x)))
         condense = jnp.where(lanes32 < active, 0.5 * soft, 0.0)
         high = condense.astype(bf16)
@@ -356,16 +354,11 @@
     sums = [jnp.zeros((8, LEV), f32) for _ in range(8)]
     for place in range(16):
         at = slice(place * ELEMS, (place + 1) * ELEMS)
-        n = ORDER[place]
         active = cols[0, :, place_lanes(place)]
         owner = cols[1, :, place_lanes(place)]
         condense = condf[at, :]
         net = condense - jnp.where(lanes32 < active, evap_rate * flux[at, :], 0.0)
-        warming, drying = latent * net, -net
-        for k in range(4):
-            spot = pl.ds(k * 128 + n, 8, stride=16)
-            tbuf[0, spot, :] = warming[8 * k : 8 * k + 8]
-            tbuf[1, spot, :] = drying[8 * k : 8 * k + 8]
+        condf[at, :] = net
         for g in range(8):
             share = jnp.where(owner == float(g), net, 0.0)
             sums[g] = sums[g] + (share[0:8] + share[8:16] + share[16:24] + share[24:32])
@@ -384,15 +377,55 @@
         copy.start()
         rain_copies.append(copy)
         started.append(copy)
+    out_field(1)
+
+    def tend_body(k, carry):
+        for n in range(16):
+            at = pl.ds(pl.multiple_of(PLACE[n] * ELEMS + k * 8, 8), 8)
+            spot = pl.ds(k * 128 + n, 8, stride=16)
+            net = condf[at, :]
+            tbuf[0, spot, :] = latent * net
+            tbuf[1, spot, :] = -net
+        return carry
+
+    lax.fori_loop(0, ELEMS // 8, tend_body, 0)
     store(tbuf, tend)
 
-    cfl[0] = jnp.sum(count_sum(3, flying))
     for copy in rain_copies:
         copy.wait_recv()
     collected = part[grp]
     for k in range(7):
         collected = collected + precv[k]
-    rain[0] = jnp.sum(collected) * np.float32(1.0 / ROWS)
+    lines[0] = collected * np.float32(1.0 / ROWS)
+
+    over_grp = [remote(cval.at[1], gsum.at[k], gs_sem.at[k], gr_sem.at[k], peer) for k, peer in enumerate(grp_peers)]
+    back = [remote(cval.at[2], ctot.at[0], gs_sem.at[6 + k], cr_sem.at[1], peer) for k, peer in enumerate(z_line, 1)]
+
+    @pl.when(is_root)
+    def _():
+        rest = crecv.at[pl.ds(1, 4 * Z_CHIPS - 1)]
+        remote(rest, rest, cs_sem.at[0], cr_sem.at[0], (nxt, grp)).wait_recv()
+        total = jnp.sum(crecv[...], axis=0)
+        cval[1] = total
+        for copy in over_grp:
+            copy.start()
+        for copy in over_grp:
+            copy.wait_recv()
+        total = total + jnp.sum(gsum[...], axis=0)
+        cval[2] = total
+        for copy in back:
+            copy.start()
+        ctot[0] = total
+        for copy in over_grp + back:
+            copy.wait_send()
+
+    @pl.when(z != ROOT)
+    def _():
+        back[0].wait_recv()
+        to_root[0].wait_send()
+
+    lines[1] = ctot[0]
+    store(lines, sums_out)
     for copy in started:
         copy.wait_send()
     for copy in stores:
@@ -402,6 +435,23 @@
 def place_lanes(place):
     n = ORDER[place]
     return slice(n * LEV, (n + 1) * LEV)
+
+
+def hand_over(dyn, tend, sums, dyn_out, tend_out, rain_out, cfl_out, lines, sem):
+    small = pltpu.make_async_copy(sums, lines, sem.at[8])
+    small.start()
+    copies = []
+    for src, dst in ((dyn, dyn_out), (tend, tend_out)):
+        for f in range(2):
+            for k in range(2):
+                at = pl.ds(k * 256, 256)
+                copies.append(pltpu.make_async_copy(src.at[f, at], dst.at[f, at], sem.at[len(copies)]))
+                copies[-1].start()
+    small.wait()
+    rain_out[0] = jnp.sum(lines[0])
+    cfl_out[0] = jnp.sum(lines[1])
+    for copy in copies:
+        copy.wait()
 
 
 def shards(prognostic, wind_field, nbr_slot, nbr_edge, flip_edge, span_dest, wet_layers_present):
@@ -411,16 +461,15 @@
     vmem = pltpu.VMEM
     dma = pltpu.SemaphoreType.DMA
     whole = (2, ROWS, LEV)
-    fields, tendency, rain, cfl = pl.pallas_call(
+    fields, tendency, sums = pl.pallas_call(
         kernel,
         out_shape=(
             jax.ShapeDtypeStruct(whole, f32),
             jax.ShapeDtypeStruct(whole, f32),
-            jax.ShapeDtypeStruct((1,), f32),
-            jax.ShapeDtypeStruct((1,), f32),
+            jax.ShapeDtypeStruct((2, 1, LEV), f32),
         ),
-        in_specs=[anywhere] * 7,
-        out_specs=(anywhere, anywhere, scalar, scalar),
+        in_specs=[pl.BlockSpec(memory_space=pltpu.HBM)] * 7,
+        out_specs=(anywhere, anywhere, anywhere),
         scratch_shapes=[
             vmem(whole, f32),
             vmem(whole, f32),
@@ -443,21 +492,26 @@
             vmem((ROWS, LEV), f32),
             vmem(whole, f32),
             vmem(whole, f32),
-            vmem((4, 1, LEV), f32),
-            vmem((20, 1, LEV), f32),
+            vmem((3, 1, LEV), f32),
+            vmem((4 * Z_CHIPS, 1, LEV), f32),
+            vmem((7, 1, LEV), f32),
+            vmem((1, 1, LEV), f32),
             vmem((8, 1, LEV), f32),
             vmem((7, 1, LEV), f32),
-            dma((8,)),
+            vmem((2, 1, LEV), f32),
+            dma((13,)),
             dma((2, 2, 2)),
             dma((2, 2, 2)),
-            dma((20,)),
-            dma((20,)),
+            dma((4,)),
+            dma((2,)),
+            dma((38,)),
             dma((7,)),
             dma((7,)),
-            dma((3,)),
+            dma((7,)),
+            dma((4,)),
         ],
         compiler_params=pltpu.CompilerParams(
-            collective_id=0, has_side_effects=True, vmem_limit_bytes=48 * 1024 * 1024
+            collective_id=0, has_side_effects=True, vmem_limit_bytes=52 * 1024 * 1024 + 655360
         ),
         cost_estimate=pl.CostEstimate(flops=2_000_000_000, bytes_accessed=2_200_000, transcendentals=200_000),
         name="steps_and_columns",
@@ -470,6 +524,20 @@
         span_dest.reshape(4, LEV),
         wet_layers_present.reshape(4, LEV),
     )
+    fields, tendency, rain, cfl = pl.pallas_call(
+        hand_over,
+        out_shape=(
+            jax.ShapeDtypeStruct(whole, f32),
+            jax.ShapeDtypeStruct(whole, f32),
+            jax.ShapeDtypeStruct((1,), f32),
+            jax.ShapeDtypeStruct((1,), f32),
+        ),
+        in_specs=[anywhere, anywhere, anywhere],
+        out_specs=(anywhere, anywhere, scalar, scalar),
+        scratch_shapes=[vmem((2, 1, LEV), f32), dma((9,))],
+        compiler_params=pltpu.CompilerParams(vmem_limit_bytes=6 * 1024 * 1024),
+        name="hand_over",
+    )(fields, tendency, sums)
     shape = prognostic.shape
     return fields.reshape(shape), tendency.reshape(shape), rain, cfl.reshape(())
 

time: 65.2 us -> 50.1 us (0.77)
  Pallas kernels: 56.4 us -> 48.5 us
  local copies, waits for them, and re-layouts: 4.38 us -> 0.7 us
  between operations: 4.18 us -> 0.68 us
    pallas_call x1, Pallas kernels: 56.4 us -> 46.9 us  [shards(): pl.pallas_call(kernel, out_shape=(jax.ShapeDtypeStruct(whole, f32), jax.S...]
    unnamed x16 -> x10, local copies, waits for them, and re-layouts: 4.38 us -> 0.7 us
    pallas_call x0 -> x1, Pallas kernels: none -> 1.56 us  [shards(): pl.pallas_call(hand_over, out_shape=(jax.ShapeDtypeStruct(whole, f32), ja...]
where the time goes in v2:
time: 50.1 us; the launch traced here: 49.9 us
  Pallas kernels  48.5 us (97%)
  local copies, waits for them, and re-layouts  0.7 us (1%)
  between operations  0.68 us (1%)
    pallas_call x1, Pallas kernels, shards(): pl.pallas_call(kernel, out_shape=(jax.ShapeDtypeStruct(whole, f32), jax.S...  46.9 us
    pallas_call x1, Pallas kernels, shards(): pl.pallas_call(hand_over, out_shape=(jax.ShapeDtypeStruct(whole, f32), ja...  1.56 us

profile of v2, /device:TPU:1, one launch (start us, length us, event | category | flops | bytes accessed | tf_op | source)
XLA Modules:
  0.0 49.9 jit_solution(11277096620297784859)
XLA Ops:
  0.6 0.0 copy-start.4
  0.6 0.0 copy-start.3
  0.7 0.0 copy-start.2
  0.7 0.0 copy-start.1
  0.7 0.0 copy-start
  0.7 0.6 %copy-done.4 = s32[512]{0:T(512)S(1)} copy-done((s32[512]{0:T(512)S(1)}, s32[512]{0:T(512)}, u32[]{:S(2)}) %copy-start.4) | copy-done | bytes 2072
  1.3 0.0 copy-done.3
  1.3 0.0 copy-done.2
  1.3 0.0 copy-done.1
  1.4 0.0 copy-done
  1.4 46.9 %steps_and_columns.1 = (f32[2,512,128]{2,1,0:T(8,128)S(1)}, f32[2,512,128]{2,1,0:T(8,128)S(1)}, f32[2,1,128]{2,1,0:T(1,128)S(1)}) custom-call(f32[2,512,128]{2,1,0:T(8,128)} %bitcast.15, f32[2,512,128]{2,1,0:T(8,128)} %bitcast.16, s32[4,32]{1,0:T(4,128)S(1)} %bitcast.10, s32[4,32]{1,0:T(4,128)S(1)} %bitcast.11, s32[4,32]{1,0:T(4,128)S(1)} %bitcast.12, ...), custom_call_target="tpu_custom_call" | custom-call | flops 2000000000 | bytes 2200000 | tf_op jit(solution)/shard_map/steps_and_columns/pallas_call | solution.py:464
  48.3 1.6 %hand_over.1 = (f32[2,512,128]{2,1,0:T(8,128)}, f32[2,512,128]{2,1,0:T(8,128)}, f32[1]{0:T(128)}, f32[1]{0:T(128)}) custom-call(f32[2,512,128]{2,1,0:T(8,128)S(1)} %get-tuple-element.11.dyn, f32[2,512,128]{2,1,0:T(8,128)S(1)} %get-tuple-element.12.tend, f32[2,1,128]{2,1,0:T(1,128)S(1)} %get-tuple-element.13.sums), custom_call_target="tpu_custom_call" | custom-call | tf_op jit(solution)/shard_map/hand_over/pallas_call | solution.py:527
Async XLA Ops:
  0.6 0.7 %copy-start.4 = (s32[512]{0:T(512)S(1)}, s32[512]{0:T(512)}, u32[]{:S(2)}) copy-start(s32[512]{0:T(512)} %param.13) | copy-start | bytes 6148
  0.6 0.7 %copy-start.3 = (s32[512,1]{0,1:T(1,128)S(1)}, s32[512,1]{0,1:T(1,128)}, u32[]{:S(2)}) copy-start(s32[512,1]{0,1:T(1,128)} %param.12) | copy-start | bytes 6148
  0.7 0.7 %copy-start.2 = (s32[32,4]{0,1:T(4,128)S(1)}, s32[32,4]{0,1:T(4,128)}, u32[]{:S(2)}) copy-start(s32[32,4]{0,1:T(4,128)} %param.11) | copy-start | bytes 1540
  0.7 0.7 %copy-start.1 = (s32[32,4]{0,1:T(4,128)S(1)}, s32[32,4]{0,1:T(4,128)}, u32[]{:S(2)}) copy-start(s32[32,4]{0,1:T(4,128)} %param.10) | copy-start | bytes 1540
  0.7 0.7 %copy-start = (s32[32,4]{0,1:T(4,128)S(1)}, s32[32,4]{0,1:T(4,128)}, u32[]{:S(2)}) copy-start(s32[32,4]{0,1:T(4,128)} %param.9) | copy-start | bytes 1540

commit v3 on v2

--- a/solution.py
+++ b/solution.py
@@ -13,6 +13,7 @@
 ROWS = 512
 LEV = 128
 EDGE_ROWS = 384
+PARTS = ((0, 256), (256, 128))
 
 edge_nodes = np.array([[0, 1, 2, 3], [3, 7, 11, 15], [12, 13, 14, 15], [0, 4, 8, 12]])
 time_step = 0.02
@@ -28,7 +29,7 @@
 SIDES = {n: [(s, i) for s in range(4) for i in range(4) if edge_nodes[s][i] == n] for n in range(16)}
 
 Z_CHIPS = 32
-ROOT = 4
+ROOT = 3
 MESH = pl.DeviceIdType.MESH
 
 
@@ -55,11 +56,11 @@
     return total
 
 
-def split_rows(src, dst, rows):
+def split_rows(src, dst, rows, first=0):
     step = 64
 
     def body(k, carry):
-        at = pl.ds(pl.multiple_of(k * step, step), step)
+        at = pl.ds(pl.multiple_of(first + k * step, step), step)
         x = src[at, :]
         high = x.astype(jnp.bfloat16)
         dst[at, 0:LEV] = high
@@ -107,7 +108,7 @@
     praw, wraw, islot, iedge, iflip, idest, iwet,
     p0, p1, base, recv, jm, rhs, rhs_own, tq, bt, cols, cond, condf, obuf, tbuf,
     cval, crecv, gsum, ctot, part, precv, lines,
-    in_sem, hs_sem, hr_sem, cs_sem, cr_sem, gs_sem, gr_sem, rs_sem, rr_sem, out_sem,
+    in_sem, hs_sem, hr_sem, cs_sem, cr_sem, gs_sem, gr_sem, rs_sem, rr_sem, out_sem, word_sem,
 ):
     f32, bf16 = jnp.float32, jnp.bfloat16
     me = lax.axis_index("elem")
@@ -134,7 +135,10 @@
     def greet(peer):
         pl.semaphore_signal(barrier, inc=1, device_id=peer, device_id_type=MESH)
 
-    for peer in [(nxt, grp), (prv, grp)] + grp_peers:
+    near = [(me, lax.rem(grp + 2 * i, 8)) for i in (1, 3)]
+    core = lax.rem(grp, 2)
+    near += [(me, lax.rem(grp - core + 2 * i, 8) + 1 - core) for i in (0, 1, 3)]
+    for peer in [(nxt, grp), (prv, grp)] + near:
         greet(peer)
 
     @pl.when(is_root)
@@ -154,26 +158,25 @@
 
         lax.fori_loop(0, ELEMS // 8, body, 0)
 
-    def halo(step, src, f):
-        copies = []
-        for way, target in enumerate((nxt, prv)):
-            copies.append(
-                pltpu.make_async_remote_copy(
-                    src_ref=src.at[f, pl.ds(0, EDGE_ROWS)],
-                    dst_ref=recv.at[step, f, pl.ds(way * EDGE_ROWS, EDGE_ROWS)],
-                    send_sem=hs_sem.at[step, f, way],
-                    recv_sem=hr_sem.at[step, f, way],
-                    device_id=(target, grp),
-                    device_id_type=MESH,
-                )
+    def halo(step, src, f, part):
+        first, rows = PARTS[part]
+        return [
+            pltpu.make_async_remote_copy(
+                src_ref=src.at[f, pl.ds(first, rows)],
+                dst_ref=recv.at[step, f, pl.ds(2 * first + way * rows, rows)],
+                send_sem=hs_sem.at[step, f, 2 * part + way],
+                recv_sem=hr_sem.at[step, f, 2 * part + way],
+                device_id=(target, grp),
+                device_id_type=MESH,
             )
-        return copies
+            for way, target in enumerate((nxt, prv))
+        ]
 
     started = []
-    halos = [[halo(s, src, f) for f in range(2)] for s, src in enumerate((p0, p1))]
+    halos = [[[halo(s, src, f, p) for p in range(2)] for f in range(2)] for s, src in enumerate((p0, p1))]
 
     def send_halo(step, f):
-        for copy in halos[step][f]:
+        for copy in halos[step][f][0] + halos[step][f][1]:
             copy.start()
             started.append(copy)
 
@@ -212,7 +215,8 @@
 
     arrived(0, 2)
     pack(0)
-    pl.semaphore_wait(barrier, jnp.where(is_root, 12, 13))
+    pl.semaphore_wait(barrier, jnp.where(is_root, 10, 11))
+    pl.semaphore_signal(word_sem, inc=1, device_id=near[1], device_id_type=MESH)
 
     @pl.when(z != ROOT)
     def _():
@@ -230,8 +234,7 @@
 
     arrived(8, 13)
     s_, e_, f_ = islot[...], iedge[...], iflip[...]
-    origin = jnp.where(s_ < ELEMS, 0, jnp.where(s_ < 2 * ELEMS, 2 * EDGE_ROWS, EDGE_ROWS))
-    origin = origin + (s_ & (ELEMS - 1))
+    is_prev, is_own = s_ < ELEMS, jnp.logical_and(s_ >= ELEMS, s_ < 2 * ELEMS)
     facing = []
     for i in range(4):
         place = jnp.full(e_.shape, EDGE_PLACE[0][i], jnp.int32)
@@ -240,7 +243,11 @@
         facing.append(place)
     tq[...] = jnp.zeros_like(tq)
     for i in range(4):
-        target = origin + ELEMS * jnp.where(f_ == 1, facing[3 - i], facing[i])
+        row = (s_ & (ELEMS - 1)) + ELEMS * jnp.where(f_ == 1, facing[3 - i], facing[i])
+        late = row >= PARTS[1][0]
+        from_prev = row + jnp.where(late, 256, 0)
+        from_next = row + jnp.where(late, 384, 256)
+        target = jnp.where(is_prev, from_prev, jnp.where(is_own, row + 2 * EDGE_ROWS, from_next))
         low = target & (LEV - 1)
         tq[4 * i : 4 * i + 4, 0:ELEMS] = (target - low).astype(f32)
         tq[16 + 4 * i : 20 + 4 * i, 0:ELEMS] = low.astype(f32)
@@ -274,12 +281,16 @@
         got = jnp.dot(jm[:, 2 * EDGE_ROWS :], rhs_own[...], preferred_element_type=f32)
         base[f, 0:EDGE_ROWS, :] = base[f, 0:EDGE_ROWS, :] + edge_scale * (got[:, :LEV] + got[:, LEV:])
 
-    def from_halo(step, f):
-        for copy in halos[step][f]:
-            copy.wait_recv()
-        split_rows(recv.at[step, f], rhs, 2 * EDGE_ROWS)
-        got = jnp.dot(jm[:, : 2 * EDGE_ROWS], rhs[...], preferred_element_type=f32)
-        return edge_scale * (got[:, :LEV] + got[:, LEV:])
+    def add_halo(step, f, dst):
+        total = base
+        for part, (first, rows) in enumerate(PARTS):
+            for copy in halos[step][f][part]:
+                copy.wait_recv()
+            split_rows(recv.at[step, f], rhs, 2 * rows, 2 * first)
+            at = slice(2 * first, 2 * (first + rows))
+            got = jnp.dot(jm[:, at], rhs[at, :], preferred_element_type=f32)
+            dst[f, 0:EDGE_ROWS, :] = total[f, 0:EDGE_ROWS, :] + edge_scale * (got[:, :LEV] + got[:, LEV:])
+            total = dst
 
     add_own(p0, 0)
     local_step(p0, wraw, base, 1)
@@ -297,7 +308,7 @@
         cols[j] = jnp.dot(tq[...].astype(bf16), spread, preferred_element_type=f32)
 
     for f in range(2):
-        p1[f, 0:EDGE_ROWS, :] = base[f, 0:EDGE_ROWS, :] + from_halo(0, f)
+        add_halo(0, f, p1)
         send_halo(1, f)
         p1[f, EDGE_ROWS:, :] = base[f, EDGE_ROWS:, :]
         if f == 0:
@@ -326,7 +337,7 @@
         lax.fori_loop(0, ELEMS // 8, body, 0)
         store(obuf.at[f], dyn.at[f])
 
-    base[0, 0:EDGE_ROWS, :] = base[0, 0:EDGE_ROWS, :] + from_halo(1, 0)
+    add_halo(1, 0, base)
     out_field(0)
 
     def threshold(k, carry):
@@ -335,37 +346,45 @@
         return carry
 
     lax.fori_loop(0, ROWS // 32, threshold, 0)
-    base[1, 0:EDGE_ROWS, :] = base[1, 0:EDGE_ROWS, :] + from_halo(1, 1)
-
-    for place in range(16):
-        at = slice(place * ELEMS, (place + 1) * ELEMS)
-        active = cols[0, :, place_lanes(place)]
-        x = 2.0 * base[1, at, :] - condf[at, :]
-        soft = jnp.maximum(x, 0.0) + jnp.log1p(jnp.exp(-jnp.abs(x)))
-        condense = jnp.where(lanes32 < active, 0.5 * soft, 0.0)
-        high = condense.astype(bf16)
-        condf[at, :] = condense
-        cond[at, 0:LEV] = high
-        cond[at, LEV:] = (condense - high.astype(f32)).astype(bf16)
+
     deep = (2 * LEV, LEV)
     above = (lax.broadcasted_iota(jnp.int32, deep, 0) & (LEV - 1)) > lax.broadcasted_iota(jnp.int32, deep, 1)
     above = jnp.where(above, 1.0, 0.0).astype(bf16)
-    flux = jnp.dot(cond[...], above, preferred_element_type=f32)
-    sums = [jnp.zeros((8, LEV), f32) for _ in range(8)]
-    for place in range(16):
-        at = slice(place * ELEMS, (place + 1) * ELEMS)
-        active = cols[0, :, place_lanes(place)]
-        owner = cols[1, :, place_lanes(place)]
-        condense = condf[at, :]
-        net = condense - jnp.where(lanes32 < active, evap_rate * flux[at, :], 0.0)
-        condf[at, :] = net
-        for g in range(8):
-            share = jnp.where(owner == float(g), net, 0.0)
-            sums[g] = sums[g] + (share[0:8] + share[8:16] + share[16:24] + share[24:32])
+
+    def columns(places, sums):
+        for place in places:
+            at = slice(place * ELEMS, (place + 1) * ELEMS)
+            active = cols[0, :, place_lanes(place)]
+            x = 2.0 * base[1, at, :] - condf[at, :]
+            soft = jnp.maximum(x, 0.0) + jnp.log1p(jnp.exp(-jnp.abs(x)))
+            condense = jnp.where(lanes32 < active, 0.5 * soft, 0.0)
+            high = condense.astype(bf16)
+            condf[at, :] = condense
+            cond[at, 0:LEV] = high
+            cond[at, LEV:] = (condense - high.astype(f32)).astype(bf16)
+        low = places[0] * ELEMS
+        flux = jnp.dot(cond[low : low + len(places) * ELEMS, :], above, preferred_element_type=f32)
+        for i, place in enumerate(places):
+            at = slice(place * ELEMS, (place + 1) * ELEMS)
+            active = cols[0, :, place_lanes(place)]
+            owner = cols[1, :, place_lanes(place)]
+            evaporate = jnp.where(lanes32 < active, evap_rate * flux[i * ELEMS : (i + 1) * ELEMS, :], 0.0)
+            net = condf[at, :] - evaporate
+            condf[at, :] = net
+            for g in range(8):
+                share = jnp.where(owner == float(g), net, 0.0)
+                sums[g] = sums[g] + (share[0:8] + share[8:16] + share[16:24] + share[24:32])
+        return sums
+
+    sums = columns(range(12, 16), [jnp.zeros((8, LEV), f32) for _ in range(8)])
+    add_halo(1, 1, base)
+    sums = columns(range(12), sums)
     for g in range(8):
         part[g] = sum_rows(sums[g])
+    pl.semaphore_wait(word_sem, 1)
     rain_copies = []
-    for k, (_, peer) in enumerate(grp_peers):
+    for k in (3, 2, 4, 1, 5, 0, 6):
+        peer = grp_peers[k][1]
         copy = pltpu.make_async_remote_copy(
             src_ref=part.at[peer],
             dst_ref=precv.at[k],
@@ -393,13 +412,12 @@
 
     for copy in rain_copies:
         copy.wait_recv()
-    collected = part[grp]
-    for k in range(7):
-        collected = collected + precv[k]
+    collected = part[grp] + jnp.sum(precv[...], axis=0)
     lines[0] = collected * np.float32(1.0 / ROWS)
 
     over_grp = [remote(cval.at[1], gsum.at[k], gs_sem.at[k], gr_sem.at[k], peer) for k, peer in enumerate(grp_peers)]
     back = [remote(cval.at[2], ctot.at[0], gs_sem.at[6 + k], cr_sem.at[1], peer) for k, peer in enumerate(z_line, 1)]
+    back = back[-ROOT:] + back[:-ROOT]
 
     @pl.when(is_root)
     def _():
@@ -500,8 +518,8 @@
             vmem((7, 1, LEV), f32),
             vmem((2, 1, LEV), f32),
             dma((13,)),
-            dma((2, 2, 2)),
-            dma((2, 2, 2)),
+            dma((2, 2, 4)),
+            dma((2, 2, 4)),
             dma((4,)),
             dma((2,)),
             dma((38,)),
@@ -509,6 +527,7 @@
             dma((7,)),
             dma((7,)),
             dma((4,)),
+            pltpu.SemaphoreType.REGULAR,
         ],
         compiler_params=pltpu.CompilerParams(
             collective_id=0, has_side_effects=True, vmem_limit_bytes=52 * 1024 * 1024 + 655360

time: 50.1 us -> 49.8 us (level)
  no operation moved by 1% of the time
where the time goes in v3:
time: 49.8 us; the launch traced here: 49.6 us
  Pallas kernels  48.2 us (97%)
  local copies, waits for them, and re-layouts  0.7 us (1%)
  between operations  0.68 us (1%)
    pallas_call x1, Pallas kernels, shards(): pl.pallas_call(kernel, out_shape=(jax.ShapeDtypeStruct(whole, f32), jax.S...  46.7 us
    pallas_call x1, Pallas kernels, shards(): pl.pallas_call(hand_over, out_shape=(jax.ShapeDtypeStruct(whole, f32), ja...  1.56 us

profile of v3, /device:TPU:1, one launch (start us, length us, event | category | flops | bytes accessed | tf_op | source)
XLA Modules:
  0.0 49.6 jit_solution(13117169476859909822)
XLA Ops:
  0.6 0.0 copy-start.4
  0.6 0.0 copy-start.3
  0.7 0.0 copy-start.2
  0.7 0.0 copy-start.1
  0.7 0.0 copy-start
  0.7 0.6 %copy-done.4 = s32[512]{0:T(512)S(1)} copy-done((s32[512]{0:T(512)S(1)}, s32[512]{0:T(512)}, u32[]{:S(2)}) %copy-start.4) | copy-done | bytes 2072
  1.3 0.0 copy-done.3
  1.3 0.0 copy-done.2
  1.3 0.0 copy-done.1
  1.4 0.0 copy-done
  1.4 46.7 %steps_and_columns.1 = (f32[2,512,128]{2,1,0:T(8,128)S(1)}, f32[2,512,128]{2,1,0:T(8,128)S(1)}, f32[2,1,128]{2,1,0:T(1,128)S(1)}) custom-call(f32[2,512,128]{2,1,0:T(8,128)} %bitcast.15, f32[2,512,128]{2,1,0:T(8,128)} %bitcast.16, s32[4,32]{1,0:T(4,128)S(1)} %bitcast.10, s32[4,32]{1,0:T(4,128)S(1)} %bitcast.11, s32[4,32]{1,0:T(4,128)S(1)} %bitcast.12, ...), custom_call_target="tpu_custom_call" | custom-call | flops 2000000000 | bytes 2200000 | tf_op jit(solution)/shard_map/steps_and_columns/pallas_call | solution.py:482
  48.0 1.6 %hand_over.1 = (f32[2,512,128]{2,1,0:T(8,128)}, f32[2,512,128]{2,1,0:T(8,128)}, f32[1]{0:T(128)}, f32[1]{0:T(128)}) custom-call(f32[2,512,128]{2,1,0:T(8,128)S(1)} %get-tuple-element.11.dyn, f32[2,512,128]{2,1,0:T(8,128)S(1)} %get-tuple-element.12.tend, f32[2,1,128]{2,1,0:T(1,128)S(1)} %get-tuple-element.13.sums), custom_call_target="tpu_custom_call" | custom-call | tf_op jit(solution)/shard_map/hand_over/pallas_call | solution.py:546
Async XLA Ops:
  0.6 0.7 %copy-start.4 = (s32[512]{0:T(512)S(1)}, s32[512]{0:T(512)}, u32[]{:S(2)}) copy-start(s32[512]{0:T(512)} %param.13) | copy-start | bytes 6148
  0.6 0.7 %copy-start.3 = (s32[512,1]{0,1:T(1,128)S(1)}, s32[512,1]{0,1:T(1,128)}, u32[]{:S(2)}) copy-start(s32[512,1]{0,1:T(1,128)} %param.12) | copy-start | bytes 6148
  0.7 0.7 %copy-start.2 = (s32[32,4]{0,1:T(4,128)S(1)}, s32[32,4]{0,1:T(4,128)}, u32[]{:S(2)}) copy-start(s32[32,4]{0,1:T(4,128)} %param.11) | copy-start | bytes 1540
  0.7 0.7 %copy-start.1 = (s32[32,4]{0,1:T(4,128)S(1)}, s32[32,4]{0,1:T(4,128)}, u32[]{:S(2)}) copy-start(s32[32,4]{0,1:T(4,128)} %param.10) | copy-start | bytes 1540
  0.7 0.7 %copy-start = (s32[32,4]{0,1:T(4,128)S(1)}, s32[32,4]{0,1:T(4,128)}, u32[]{:S(2)}) copy-start(s32[32,4]{0,1:T(4,128)} %param.9) | copy-start | bytes 1540

commit v4 on v3

--- a/solution.py
+++ b/solution.py
@@ -13,7 +13,7 @@
 ROWS = 512
 LEV = 128
 EDGE_ROWS = 384
-PARTS = ((0, 256), (256, 128))
+PARTS = ((0, EDGE_ROWS),)
 
 edge_nodes = np.array([[0, 1, 2, 3], [3, 7, 11, 15], [12, 13, 14, 15], [0, 4, 8, 12]])
 time_step = 0.02
@@ -29,7 +29,7 @@
 SIDES = {n: [(s, i) for s in range(4) for i in range(4) if edge_nodes[s][i] == n] for n in range(16)}
 
 Z_CHIPS = 32
-ROOT = 3
+ROOT = 4
 MESH = pl.DeviceIdType.MESH
 
 
@@ -173,10 +173,10 @@
         ]
 
     started = []
-    halos = [[[halo(s, src, f, p) for p in range(2)] for f in range(2)] for s, src in enumerate((p0, p1))]
+    halos = [[[halo(s, src, f, p) for p in range(len(PARTS))] for f in range(2)] for s, src in enumerate((p0, p1))]
 
     def send_halo(step, f):
-        for copy in halos[step][f][0] + halos[step][f][1]:
+        for copy in sum(halos[step][f], []):
             copy.start()
             started.append(copy)
 
@@ -244,10 +244,7 @@
     tq[...] = jnp.zeros_like(tq)
     for i in range(4):
         row = (s_ & (ELEMS - 1)) + ELEMS * jnp.where(f_ == 1, facing[3 - i], facing[i])
-        late = row >= PARTS[1][0]
-        from_prev = row + jnp.where(late, 256, 0)
-        from_next = row + jnp.where(late, 384, 256)
-        target = jnp.where(is_prev, from_prev, jnp.where(is_own, row + 2 * EDGE_ROWS, from_next))
+        target = row + jnp.where(is_prev, 0, jnp.where(is_own, 2 * EDGE_ROWS, EDGE_ROWS))
         low = target & (LEV - 1)
         tq[4 * i : 4 * i + 4, 0:ELEMS] = (target - low).astype(f32)
         tq[16 + 4 * i : 20 + 4 * i, 0:ELEMS] = low.astype(f32)
@@ -518,8 +515,8 @@
             vmem((7, 1, LEV), f32),
             vmem((2, 1, LEV), f32),
             dma((13,)),
-            dma((2, 2, 4)),
-            dma((2, 2, 4)),
+            dma((2, 2, 2)),
+            dma((2, 2, 2)),
             dma((4,)),
             dma((2,)),
             dma((38,)),

time: 49.8 us -> 49.9 us (level)
  no operation moved by 1% of the time
where the time goes in v4:
time: 49.9 us; the launch traced here: 49.7 us
  Pallas kernels  48.3 us (97%)
  local copies, waits for them, and re-layouts  0.7 us (1%)
  between operations  0.68 us (1%)
    pallas_call x1, Pallas kernels, shards(): pl.pallas_call(kernel, out_shape=(jax.ShapeDtypeStruct(whole, f32), jax.S...  46.8 us
    pallas_call x1, Pallas kernels, shards(): pl.pallas_call(hand_over, out_shape=(jax.ShapeDtypeStruct(whole, f32), ja...  1.56 us

profile of v4, /device:TPU:1, one launch (start us, length us, event | category | flops | bytes accessed | tf_op | source)
XLA Modules:
  0.0 49.7 jit_solution(15574720766046542572)
XLA Ops:
  0.6 0.0 copy-start.4
  0.6 0.0 copy-start.3
  0.7 0.0 copy-start.2
  0.7 0.0 copy-start.1
  0.7 0.0 copy-start
  0.7 0.6 %copy-done.4 = s32[512]{0:T(512)S(1)} copy-done((s32[512]{0:T(512)S(1)}, s32[512]{0:T(512)}, u32[]{:S(2)}) %copy-start.4) | copy-done | bytes 2072
  1.3 0.0 copy-done.3
  1.3 0.0 copy-done.2
  1.3 0.0 copy-done.1
  1.4 0.0 copy-done
  1.4 46.8 %steps_and_columns.1 = (f32[2,512,128]{2,1,0:T(8,128)S(1)}, f32[2,512,128]{2,1,0:T(8,128)S(1)}, f32[2,1,128]{2,1,0:T(1,128)S(1)}) custom-call(f32[2,512,128]{2,1,0:T(8,128)} %bitcast.15, f32[2,512,128]{2,1,0:T(8,128)} %bitcast.16, s32[4,32]{1,0:T(4,128)S(1)} %bitcast.10, s32[4,32]{1,0:T(4,128)S(1)} %bitcast.11, s32[4,32]{1,0:T(4,128)S(1)} %bitcast.12, ...), custom_call_target="tpu_custom_call" | custom-call | flops 2000000000 | bytes 2200000 | tf_op jit(solution)/shard_map/steps_and_columns/pallas_call | solution.py:479
  48.2 1.6 %hand_over.1 = (f32[2,512,128]{2,1,0:T(8,128)}, f32[2,512,128]{2,1,0:T(8,128)}, f32[1]{0:T(128)}, f32[1]{0:T(128)}) custom-call(f32[2,512,128]{2,1,0:T(8,128)S(1)} %get-tuple-element.11.dyn, f32[2,512,128]{2,1,0:T(8,128)S(1)} %get-tuple-element.12.tend, f32[2,1,128]{2,1,0:T(1,128)S(1)} %get-tuple-element.13.sums), custom_call_target="tpu_custom_call" | custom-call | tf_op jit(solution)/shard_map/hand_over/pallas_call | solution.py:543
Async XLA Ops:
  0.6 0.7 %copy-start.4 = (s32[512]{0:T(512)S(1)}, s32[512]{0:T(512)}, u32[]{:S(2)}) copy-start(s32[512]{0:T(512)} %param.13) | copy-start | bytes 6148
  0.6 0.7 %copy-start.3 = (s32[512,1]{0,1:T(1,128)S(1)}, s32[512,1]{0,1:T(1,128)}, u32[]{:S(2)}) copy-start(s32[512,1]{0,1:T(1,128)} %param.12) | copy-start | bytes 6148
  0.7 0.7 %copy-start.2 = (s32[32,4]{0,1:T(4,128)S(1)}, s32[32,4]{0,1:T(4,128)}, u32[]{:S(2)}) copy-start(s32[32,4]{0,1:T(4,128)} %param.11) | copy-start | bytes 1540
  0.7 0.7 %copy-start.1 = (s32[32,4]{0,1:T(4,128)S(1)}, s32[32,4]{0,1:T(4,128)}, u32[]{:S(2)}) copy-start(s32[32,4]{0,1:T(4,128)} %param.10) | copy-start | bytes 1540
  0.7 0.7 %copy-start = (s32[32,4]{0,1:T(4,128)S(1)}, s32[32,4]{0,1:T(4,128)}, u32[]{:S(2)}) copy-start(s32[32,4]{0,1:T(4,128)} %param.9) | copy-start | bytes 1540
